TPU v7x, 512 devices: a whole 4x8x8 slice. The times are simulated.
512 devices in a mesh: grp: 16 (over y, core), shard: 32 (over x, z).
Axes of the slice: x: 4, y: 8, z: 8, core: 2. Of those that a mesh axis runs over, the one named last changes fastest.
Arguments:
- table: float32 [32768, 64], P('shard'), may hold values from -6 to 6
- accum: float32 [32768, 64], P('shard'), may hold values from 0.1 to 10
- grad_values: float32 [65536, 64], P(('grp', 'shard')), may hold values from -6 to 6
- grad_rows: int32 [65536], P(('grp', 'shard')), may hold values from 0 to 1023
- grad_counts: int32 [16384], P(('grp', 'shard')), may hold values from 1 to 4
- bucket_ids: int32 [131072, 24, 2], P(('grp', 'shard')), may hold values from 0 to 32767, as said below
- bag_lengths: int32 [131072, 24], P(('grp', 'shard')), may hold values from 1 to 2
- w_hidden: bfloat16 [1536, 1024], P('shard'), may hold values from -0.15625 to 0.15625
- b_hidden: float32 [1024], replicated, may hold values from -3 to 3
- w_score: bfloat16 [1024], replicated, may hold values from -0.1875 to 0.1875
Outputs:
- table_out: float32 [32768, 64], P('shard')
- accum_out: float32 [32768, 64], P('shard')
- scores: float32 [131072], P(('grp', 'shard'))
Inputs may be any that keep to these rules, and one draw needn't show every extreme that they name: `bucket_ids`: counting all 24 x 2 id slots of a device's 256 requests, also those past a bag's length, and calling id // 1024 the owner: one owner gets exactly 768 of them, the same owner for every device of one group along grp, and every other owner's count differs from the others' by at most one.
All inputs are finite; a program needn't handle non-finite values.
Results may differ from a plain program's by a relative error of at most 0.0054.
Values may be sent and summed in bfloat16 or wider, within the bound.
No kernel may reach another device: no remote copies, remote signals or barrier semaphores. Data moves between devices by JAX's collectives and lax.ppermute only.
A program may use at most 64 MiB of HBM per device.

v0:
```python
import math
import jax
import jax.numpy as jnp
from jax import lax
from jax.sharding import PartitionSpec as P


def sum_into_rows(row_count, target_rows, slot_values):
    picks = (jnp.arange(row_count, dtype=jnp.int32)[:, None] == target_rows[None, :]).astype(
        jnp.float32
    )
    return jnp.dot(
        picks, slot_values, precision=lax.Precision.HIGHEST, preferred_element_type=jnp.float32
    )


def build_requests(owner_pick, within, local_rows, capacity):
    owner_total = owner_pick.shape[1]
    within_pick = (within[:, None] == jnp.arange(capacity, dtype=jnp.int32)[None, :]).astype(
        jnp.bfloat16
    )
    low_part = (local_rows % 256).astype(jnp.float32)
    high_part = (local_rows // 256).astype(jnp.float32)
    left_side = jnp.concatenate(
        [owner_pick * low_part[:, None], owner_pick * high_part[:, None]], axis=1
    ).astype(jnp.bfloat16)
    packed = jnp.einsum("sk,sc->kc", left_side, within_pick, preferred_element_type=jnp.float32)
    return (packed[owner_total:] * 256.0 + packed[:owner_total]).astype(jnp.int32)


def per_device(
    table,
    accum,
    grad_values,
    grad_rows,
    grad_counts,
    bucket_ids,
    bag_lengths,
    w_hidden,
    b_hidden,
    w_score,
):
    shard_count = lax.axis_size("shard")
    rows_here, row_width = table.shape
    slot_rows = grad_rows.shape[0] // shard_count
    live_rows = jnp.arange(slot_rows, dtype=jnp.int32)[None, :] < grad_counts[:, None]
    grad_slots = jnp.where(
        live_rows[:, :, None], grad_values.reshape(shard_count, slot_rows, row_width), 0.0
    )
    targets = grad_rows.reshape(shard_count, slot_rows)
    got_values, got_rows = (
        lax.all_to_all(grad_slots, "shard", split_axis=0, concat_axis=0, tiled=True),
        lax.all_to_all(targets, "shard", split_axis=0, concat_axis=0, tiled=True),
    )
    owned_sum = sum_into_rows(rows_here, got_rows.reshape(-1), got_values.reshape(-1, row_width))
    grad_sum = lax.psum(owned_sum, "grp")
    accum_out = accum + grad_sum * grad_sum
    table_out = table - 0.5 * grad_sum * lax.rsqrt(accum_out)
    serving_rows = table_out.astype(jnp.bfloat16)
    request_count, vocab_count, bag_size = bucket_ids.shape
    flat_ids = bucket_ids.reshape(-1)
    slot_count = flat_ids.shape[0]
    capacity = 2 * slot_count // shard_count
    owners = flat_ids // rows_here
    local_rows = flat_ids % rows_here
    owner_iota = jnp.arange(shard_count, dtype=jnp.int32)
    block_len = math.gcd(slot_count, 256)
    block_total = slot_count // block_len
    owner_hot = (
        owners.reshape(block_total, block_len)[:, :, None] == owner_iota[None, None, :]
    ).astype(jnp.bfloat16)
    position = jnp.arange(block_len, dtype=jnp.int32)
    lower_ones = (position[:, None] >= position[None, :]).astype(jnp.bfloat16)
    inclusive = jnp.einsum("ij,bjk->bik", lower_ones, owner_hot, preferred_element_type=jnp.float32)
    owner_float = owner_hot.astype(jnp.float32)
    block_sums = jnp.sum(owner_float, axis=1)
    block_offsets = jnp.cumsum(block_sums, axis=0) - block_sums
    ranks = inclusive + block_offsets[:, None, :]
    within = (jnp.sum(owner_float * ranks, axis=2) - 1.0).reshape(-1).astype(jnp.int32)
    owner_pick = owner_float.reshape(slot_count, shard_count)
    placed = owners * capacity + within
    requested = build_requests(owner_pick, within, local_rows, capacity)
    fetched = serving_rows[
        lax.all_to_all(requested, "shard", split_axis=0, concat_axis=0, tiled=True)
    ]
    returned = lax.all_to_all(fetched, "shard", split_axis=0, concat_axis=0, tiled=True)
    own_rows = returned.reshape(shard_count * capacity, row_width)[placed]
    own_rows = own_rows.reshape(request_count, vocab_count, bag_size, row_width)
    in_bag = jnp.arange(bag_size, dtype=jnp.int32)[None, None, :] < bag_lengths[:, :, None]
    pooled = jnp.sum(jnp.where(in_bag[..., None], own_rows.astype(jnp.float32), 0.0), axis=2)
    pooled = pooled.astype(jnp.bfloat16).reshape(request_count, vocab_count * row_width)
    hidden_pre = jnp.dot(
        pooled,
        lax.all_gather(w_hidden, "shard", axis=0, tiled=True),
        preferred_element_type=jnp.float32,
    )
    hidden = jax.nn.silu(hidden_pre + b_hidden).astype(jnp.bfloat16)
    scores = jnp.dot(hidden, w_score, preferred_element_type=jnp.float32)
    return (table_out, accum_out, scores)


def solution(mesh):
    return jax.shard_map(
        per_device,
        mesh=mesh,
        in_specs=(
            P("shard", None),
            P("shard", None),
            P(("grp", "shard"), None),
            P(("grp", "shard")),
            P(("grp", "shard")),
            P(("grp", "shard"), None, None),
            P(("grp", "shard"), None),
            P("shard", None),
            P(),
            P(),
        ),
        out_specs=(P("shard", None), P("shard", None), P(("grp", "shard"))),
        check_vma=False,
    )
```

profile of v0, /device:TPU:6, one launch (start us, length us, event | category | flops | bytes accessed | tf_op | source)
XLA Modules:
  0.0 444.5 jit_solution(10169167343859944870)
XLA Ops:
  8.0 1.4 all_to_all.20
  9.4 13.4 %all-to-all-start = ((s32[32,1,4]{2,1,0:T(1,128)}), s32[32,1,4]{2,1,0:T(1,128)S(1)}, u32[]{:S(2)}, u32[]{:S(2)}) async-start(s32[32,1,4]{2,1,0:T(1,128)} %bitcast), calls=%async_computation | async-start | bytes 32768 | tf_op jit(solution)/shard_map/all_to_all | solution.py:53
  22.8 1.8 copy.46
  24.7 2.1 reshape.301
  26.8 2.1 reshape.302
  29.4 0.7 fusion.5
  30.1 0.6 convert_bitcast_fusion
  31.2 7.7 %fusion = f32[64,768]{1,0:T(8,128)S(1)} fusion(s32[12288]{0:T(1024)S(1)} %bitcast.41, bf16[12288,32]{0,1:T(8,128)(2,1)S(1)} %get-tuple-element.9, bf16[12288,32]{0,1:T(8,128)(2,1)S(1)} %get-tuple-element.8), kind=kOutput, calls=%fused_computation.3 | convolution fusion | flops 1220542464 | bytes 1818624 | tf_op jit(solution)/shard_map/sk,sc->kc/dot_general | solution.py:27
  39.0 0.7 reshape.335
  39.7 9.8 %all-to-all-start.1 = ((f32[32,1,256]{2,1,0:T(1,128)}), f32[32,1,256]{2,1,0:T(1,128)S(1)}, u32[]{:S(2)}, u32[]{:S(2)}) async-start(f32[32,1,256]{2,1,0:T(1,128)} %reshape.335), calls=%async_computation.1 | async-start | bytes 65536 | tf_op jit(solution)/shard_map/all_to_all | solution.py:52
  49.5 0.7 copy.48
  50.8 0.7 reduce.3
  51.6 6.0 %all-to-all-done.1 = f32[32,1,256]{2,1,0:T(1,128)S(1)} async-done(((f32[32,1,256]{2,1,0:T(1,128)}), f32[32,1,256]{2,1,0:T(1,128)S(1)}, u32[]{:S(2)}, u32[]{:S(2)}) %all-to-all-start.1) | async-done | bytes 32800 | tf_op jit(solution)/shard_map/all_to_all | solution.py:52
  57.5 5.7 %all-to-all-start.2 = ((s32[32,1,768]{2,1,0:T(1,128)}), s32[32,1,768]{2,1,0:T(1,128)S(1)}, u32[]{:S(2)}, u32[]{:S(2)}) async-start(s32[32,1,768]{2,1,0:T(1,128)} %copy.48), calls=%async_computation.2 | async-start | bytes 196608 | tf_op jit(solution)/shard_map/all_to_all | solution.py:84
  63.8 0.7 reduce.4
  64.7 1.1 fusion.16
  65.8 5.8 %all-to-all-done.2 = s32[32,1,768]{2,1,0:T(1,128)S(1)} async-done(((s32[32,1,768]{2,1,0:T(1,128)}), s32[32,1,768]{2,1,0:T(1,128)S(1)}, u32[]{:S(2)}, u32[]{:S(2)}) %all-to-all-start.2) | async-done | bytes 98336 | tf_op jit(solution)/shard_map/all_to_all | solution.py:84
  71.7 0.7 broadcast_clamp_fusion
  72.3 109.3 %all-reduce.2.cloned.1.call-done = f32[1024,64]{0,1:T(8,128)} async-done(((f32[1024,64]{0,1:T(8,128)}), f32[1024,64]{0,1:T(8,128)}) %all-reduce.2.cloned.1.call-update) | async-done | bytes 262160 | tf_op jit(solution)/shard_map/psum | solution.py:56
  181.7 2.0 fusion.32
  183.8 93.6 %gather_fusion = bf16[24576,64]{1,0:T(8,128)(2,1)} fusion(bf16[1024,64]{1,0:T(8,128)(2,1)S(1)} %copy.49, s32[24576]{0:T(1024)} %broadcast_clamp_fusion), kind=kCustom, calls=%fused_computation | custom fusion | bytes 6389760 | tf_op jit(solution)/shard_map/gather | solution.py:83
  277.4 6.8 %copy.50 = bf16[32,768,64]{1,2,0:T(8,128)(2,1)} copy(bf16[32,768,64]{2,1,0:T(8,128)(2,1)} %bitcast.33) | data formatting | bytes 6291456 | tf_op jit(solution)/shard_map/gather | solution.py:83
  284.3 10.6 %all-to-all-start.3 = ((bf16[32,768,64]{1,2,0:T(8,128)(2,1)}), bf16[32,768,64]{1,2,0:T(8,128)(2,1)}, u32[]{:S(2)}, u32[]{:S(2)}) async-start(bf16[32,768,64]{1,2,0:T(8,128)(2,1)} %copy.50), calls=%async_computation.3 | async-start | bytes 6291456 | tf_op jit(solution)/shard_map/all_to_all | solution.py:86
  295.0 0.5 all-gather.2.cloned.1.call-update
  295.5 2.2 reshape.304
  297.9 2.2 iota_compare_fusion.2
  300.4 72.3 %all-to-all-done.3 = bf16[32,768,64]{1,2,0:T(8,128)(2,1)} async-done(((bf16[32,768,64]{1,2,0:T(8,128)(2,1)}), bf16[32,768,64]{1,2,0:T(8,128)(2,1)}, u32[]{:S(2)}, u32[]{:S(2)}) %all-to-all-start.3) | async-done | bytes 3145760 | tf_op jit(solution)/shard_map/all_to_all | solution.py:86
  372.7 6.6 %copy.51 = bf16[32,768,64]{2,1,0:T(8,128)(2,1)} copy(bf16[32,768,64]{1,2,0:T(8,128)(2,1)} %all-to-all-done.3) | data formatting | bytes 6291456 | tf_op jit(solution)/shard_map/all_to_all | solution.py:86
  379.3 36.4 %gather_fusion.1 = bf16[12288,64]{1,0:T(8,128)(2,1)S(1)} fusion(bf16[24576,64]{1,0:T(8,128)(2,1)} %bitcast.32, s32[12288]{0:T(1024)S(1)} %broadcast_clamp_fusion.1), kind=kCustom, calls=%fused_computation.1 | custom fusion | bytes 3194880 | tf_op jit(solution)/shard_map/gather | solution.py:87
  415.8 15.5 %fusion.2 = bf16[256,24,64]{2,1,0:T(8,128)(2,1)} fusion(bf16[256,24,2,64]{3,2,1,0:T(2,128)(2,1)S(1)} %bitcast.34, pred[256,24,2]{2,1,0:T(8,128)(4,1)} %iota_compare_fusion.2), kind=kLoop, calls=%fused_computation.6 | loop fusion | flops 1966080 | bytes 2371584 | tf_op jit(solution)/shard_map/reduce_sum | solution.py:90
  431.3 2.0 copy.53
  433.3 3.7 fusion.12
  (39 shorter events, 3.2 us)
Async XLA Ops:
  9.4 30.3 %all-to-all-start = ((s32[32,1,4]{2,1,0:T(1,128)}), s32[32,1,4]{2,1,0:T(1,128)S(1)}, u32[]{:S(2)}, u32[]{:S(2)}) async-start(s32[32,1,4]{2,1,0:T(1,128)} %bitcast), calls=%async_computation | async-start | bytes 32768 | tf_op jit(solution)/shard_map/all_to_all | solution.py:53
  26.8 4.0 copy-start.1
  26.8 4.1 copy-start.4
  39.7 17.8 %all-to-all-start.1 = ((f32[32,1,256]{2,1,0:T(1,128)}), f32[32,1,256]{2,1,0:T(1,128)S(1)}, u32[]{:S(2)}, u32[]{:S(2)}) async-start(f32[32,1,256]{2,1,0:T(1,128)} %reshape.335), calls=%async_computation.1 | async-start | bytes 65536 | tf_op jit(solution)/shard_map/all_to_all | solution.py:52
  57.5 14.1 %all-to-all-start.2 = ((s32[32,1,768]{2,1,0:T(1,128)}), s32[32,1,768]{2,1,0:T(1,128)S(1)}, u32[]{:S(2)}, u32[]{:S(2)}) async-start(s32[32,1,768]{2,1,0:T(1,128)} %copy.48), calls=%async_computation.2 | async-start | bytes 196608 | tf_op jit(solution)/shard_map/all_to_all | solution.py:84
  63.3 118.4 %all-reduce.2.cloned.1.call-start = ((), (), s32[]{:S(2)}) async-start(), calls=%async_computation.4 | async-start | bytes 524288 | tf_op jit(solution)/shard_map/psum | solution.py:56
  284.3 88.4 %all-to-all-start.3 = ((bf16[32,768,64]{1,2,0:T(8,128)(2,1)}), bf16[32,768,64]{1,2,0:T(8,128)(2,1)}, u32[]{:S(2)}, u32[]{:S(2)}) async-start(bf16[32,768,64]{1,2,0:T(8,128)(2,1)} %copy.50), calls=%async_computation.3 | async-start | bytes 6291456 | tf_op jit(solution)/shard_map/all_to_all | solution.py:86
  294.9 2.8 copy-start
  294.9 2.9 copy-start.2
  294.9 3.0 copy-start.3
  294.9 138.4 %all-gather.2.cloned.1.call-start = ((), (), s32[]{:S(2)}) async-start(), calls=%async_computation.5 | async-start | bytes 3244032 | tf_op jit(solution)/shard_map/all_gather | solution.py:94
  415.8 17.6 %copy-start.5 = (f32[1024]{0:T(1024)S(1)}, f32[1024]{0:T(1024)}, u32[]{:S(2)}) copy-start(f32[1024]{0:T(1024)} %param.18) | copy-start | bytes 12292
Sparse Core Ops, SparseCore 0:
  67.0 114.6 all-reduce.1
Sparse Core Ops, SparseCore 1:
  299.0 94.9 all-gather.1
where the time goes:
time: 447 us; the launch traced here: 445 us
  waiting for transfers between devices  194 us (43%)
  local copies, waits for them, and re-layouts  158 us (35%)
  starting transfers between devices  39.6 us (9%)
  other arithmetic  23.7 us (5%)
  between operations  15.8 us (4%)
  matrix products  13.2 us (3%)
    psum x1, waiting for transfers between devices, per_device(): grad_sum = lax.psum(owned_sum, 'grp')  109 us
    gather x2, local copies, waits for them, and re-layouts, per_device(): serving_rows[lax.all_to_all(requested, 'shard', split_axis=0, concat_axis...  100 us
    all_to_all x1, waiting for transfers between devices, per_device(): lax.all_to_all(fetched, 'shard', split_axis=0, concat_axis=0, tiled=True)  72.3 us
    gather x1, local copies, waits for them, and re-layouts, per_device(): own_rows = returned.reshape(shard_count * capacity, row_width)[placed]  36.4 us
    reduce_sum x1, other arithmetic, per_device(): jnp.sum(jnp.where(in_bag[..., None], own_rows.astype(jnp.float32), 0.0),...  15.5 us
    all_to_all x1, starting transfers between devices, per_device(): lax.all_to_all(targets, 'shard', split_axis=0, concat_axis=0, tiled=True)  13.4 us
    all_to_all x1, starting transfers between devices, per_device(): lax.all_to_all(fetched, 'shard', split_axis=0, concat_axis=0, tiled=True)  10.6 us
    all_to_all x1, starting transfers between devices, per_device(): lax.all_to_all(grad_slots, 'shard', split_axis=0, concat_axis=0, tiled=True)  9.78 us
  transfers between devices with their start and end apart: 6, of which 4 were waited for; matrix products, arithmetic and copies ran while one was open for 20% of the time, Pallas kernels for 0%

commit v1 on v0

--- a/solution.py
+++ b/solution.py
@@ -53,7 +53,8 @@
         lax.all_to_all(targets, "shard", split_axis=0, concat_axis=0, tiled=True),
     )
     owned_sum = sum_into_rows(rows_here, got_rows.reshape(-1), got_values.reshape(-1, row_width))
-    grad_sum = lax.psum(owned_sum, "grp")
+    pieces = lax.all_gather(owned_sum, "grp")
+    grad_sum = jnp.sum(pieces, axis=0)
     accum_out = accum + grad_sum * grad_sum
     table_out = table - 0.5 * grad_sum * lax.rsqrt(accum_out)
     serving_rows = table_out.astype(jnp.bfloat16)

time: 447 us -> 361 us (0.81)
  waiting for transfers between devices: 194 us -> 96.5 us
  blocking collectives: 0 us -> 13.2 us
  starting transfers between devices: 39.6 us -> 29.5 us
  local copies, waits for them, and re-layouts: 158 us -> 163 us
    psum x1 -> x0, waiting for transfers between devices: 109 us -> none  [per_device(): grad_sum = lax.psum(owned_sum, 'grp')]
    all_to_all x0 -> x1, blocking collectives: none -> 13.2 us  [per_device(): lax.all_to_all(requested, 'shard', split_axis=0, concat_axis=0, tiled=True)]
    all_gather x0 -> x1, waiting for transfers between devices: none -> 11.2 us  [per_device(): pieces = lax.all_gather(owned_sum, 'grp')]
    all_to_all x1 -> x0, waiting for transfers between devices: 5.77 us -> none  [per_device(): lax.all_to_all(requested, 'shard', split_axis=0, concat_axis=0, tiled=True)]
    all_to_all x1 -> x0, starting transfers between devices: 5.74 us -> none  [per_device(): lax.all_to_all(requested, 'shard', split_axis=0, concat_axis=0, tiled=True)]
    unnamed x20 -> x21, local copies, waits for them, and re-layouts: 2.96 us -> 8.64 us
    all_to_all x1, waiting for transfers between devices: 0.01 us -> 5.41 us  [per_device(): lax.all_to_all(targets, 'shard', split_axis=0, concat_axis=0, tiled=True)]
  transfers between devices with their start and end apart: 6 -> 5, of which waited for: 4 -> 4; matrix products, arithmetic and copies ran while one was open for 20% -> 24% of each run, Pallas kernels for 0% -> 0%
where the time goes in v1:
time: 361 us; the launch traced here: 356 us
  local copies, waits for them, and re-layouts  163 us (45%)
  waiting for transfers between devices  96.5 us (27%)
  starting transfers between devices  29.5 us (8%)
  other arithmetic  24.4 us (7%)
  between operations  15.8 us (4%)
  matrix products  13.2 us (4%)
  blocking collectives  13.2 us (4%)
    gather x2, local copies, waits for them, and re-layouts, per_device(): serving_rows[lax.all_to_all(requested, 'shard', split_axis=0, concat_axis...  100 us
    all_to_all x1, waiting for transfers between devices, per_device(): lax.all_to_all(fetched, 'shard', split_axis=0, concat_axis=0, tiled=True)  72.8 us
    gather x1, local copies, waits for them, and re-layouts, per_device(): own_rows = returned.reshape(shard_count * capacity, row_width)[placed]  36.4 us
    reduce_sum x1, other arithmetic, per_device(): jnp.sum(jnp.where(in_bag[..., None], own_rows.astype(jnp.float32), 0.0),...  15.5 us
    all_to_all x1, starting transfers between devices, per_device(): lax.all_to_all(targets, 'shard', split_axis=0, concat_axis=0, tiled=True)  13.4 us
    all_to_all x1, blocking collectives, per_device(): lax.all_to_all(requested, 'shard', split_axis=0, concat_axis=0, tiled=True)  13.2 us
    all_gather x1, waiting for transfers between devices, per_device(): pieces = lax.all_gather(owned_sum, 'grp')  11.2 us
    all_to_all x1, starting transfers between devices, per_device(): lax.all_to_all(fetched, 'shard', split_axis=0, concat_axis=0, tiled=True)  10.2 us
  transfers between devices with their start and end apart: 5, of which 4 were waited for; matrix products, arithmetic and copies ran while one was open for 24% of the time, Pallas kernels for 0%

profile of v1, /device:TPU:6, one launch (start us, length us, event | category | flops | bytes accessed | tf_op | source)
XLA Modules:
  0.0 355.8 jit_solution(15437100690890184723)
XLA Ops:
  8.0 1.4 all_to_all.20
  9.4 13.4 %all-to-all-start = ((s32[32,1,4]{2,1,0:T(1,128)}), s32[32,1,4]{2,1,0:T(1,128)S(1)}, u32[]{:S(2)}, u32[]{:S(2)}) async-start(s32[32,1,4]{2,1,0:T(1,128)} %bitcast), calls=%async_computation | async-start | bytes 32768 | tf_op jit(solution)/shard_map/all_to_all | solution.py:53
  22.8 0.8 copy.62
  23.7 0.7 iota_compare_fusion.11
  24.5 0.7 reshape.336
  25.2 5.4 %all-to-all-done = s32[32,1,4]{2,1,0:T(1,128)S(1)} async-done(((s32[32,1,4]{2,1,0:T(1,128)}), s32[32,1,4]{2,1,0:T(1,128)S(1)}, u32[]{:S(2)}, u32[]{:S(2)}) %all-to-all-start) | async-done | bytes 544 | tf_op jit(solution)/shard_map/all_to_all | solution.py:53
  30.7 5.7 %all-to-all-start.1 = ((f32[32,1,256]{2,1,0:T(1,128)}), f32[32,1,256]{2,1,0:T(1,128)S(1)}, u32[]{:S(2)}, u32[]{:S(2)}) async-start(f32[32,1,256]{2,1,0:T(1,128)} %reshape.336), calls=%async_computation.1 | async-start | bytes 65536 | tf_op jit(solution)/shard_map/all_to_all | solution.py:52
  37.0 0.7 reduce.3
  37.8 6.6 %all-to-all-done.1 = f32[32,1,256]{2,1,0:T(1,128)S(1)} async-done(((f32[32,1,256]{2,1,0:T(1,128)}), f32[32,1,256]{2,1,0:T(1,128)S(1)}, u32[]{:S(2)}, u32[]{:S(2)}) %all-to-all-start.1) | async-done | bytes 32800 | tf_op jit(solution)/shard_map/all_to_all | solution.py:52
  44.8 0.7 reduce.4
  45.6 1.1 fusion.16
  46.8 2.0 copy.64
  48.8 2.1 reshape.301
  50.9 2.1 reshape.302
  53.5 0.7 fusion.5
  55.2 7.7 %fusion = f32[64,768]{1,0:T(8,128)S(1)} fusion(s32[12288]{0:T(1024)S(1)} %bitcast.47, bf16[12288,32]{0,1:T(8,128)(2,1)S(1)} %get-tuple-element.21, bf16[12288,32]{0,1:T(8,128)(2,1)S(1)} %get-tuple-element.20), kind=kOutput, calls=%fused_computation.3 | convolution fusion | flops 1220542464 | bytes 1818624 | tf_op jit(solution)/shard_map/sk,sc->kc/dot_general | solution.py:27
  63.0 13.2 %all_to_all.31 = s32[32,1,768]{2,1,0:T(1,128)S(1)} all-to-all(s32[32,1,768]{2,1,0:T(1,128)S(1)} %copy.66), channel_id=1, replica_groups=mesh['grp'=16,'shard'=32] {'shard'}, dimensions={0} | all-to-all | bytes 196608 | tf_op jit(solution)/shard_map/all_to_all | solution.py:85
  76.9 11.2 %all-gather.6.cloned.1.call-done = f32[16384,64]{0,1:T(8,128)} async-done(((f32[1024,64]{0,1:T(8,128)}), f32[16384,64]{0,1:T(8,128)}) %all-gather.6.cloned.1.call-update) | async-done | bytes 4194320 | tf_op jit(solution)/shard_map/all_gather | solution.py:56
  88.1 4.6 %copy.72 = f32[8,8,16,1024]{3,2,1,0:T(8,128)S(1)} copy(f32[8,8,16,1024]{3,1,2,0:T(8,128)} %bitcast.40) | data formatting | bytes 8388608
  92.7 0.8 bitcast_reduce_fusion
  93.7 0.8 fusion.32
  94.7 93.7 %gather_fusion = bf16[24576,64]{1,0:T(8,128)(2,1)} fusion(bf16[1024,64]{1,0:T(8,128)(2,1)S(1)} %copy.67, s32[24576]{0:T(1024)} %broadcast_clamp_fusion), kind=kCustom, calls=%fused_computation | custom fusion | bytes 6389760 | tf_op jit(solution)/shard_map/gather | solution.py:84
  188.4 6.8 %copy.68 = bf16[32,768,64]{1,2,0:T(8,128)(2,1)} copy(bf16[32,768,64]{2,1,0:T(8,128)(2,1)} %bitcast.38) | data formatting | bytes 6291456 | tf_op jit(solution)/shard_map/gather | solution.py:84
  195.2 10.2 %all-to-all-start.3 = ((bf16[32,768,64]{1,2,0:T(8,128)(2,1)}), bf16[32,768,64]{1,2,0:T(8,128)(2,1)}, u32[]{:S(2)}, u32[]{:S(2)}) async-start(bf16[32,768,64]{1,2,0:T(8,128)(2,1)} %copy.68), calls=%async_computation.3 | async-start | bytes 6291456 | tf_op jit(solution)/shard_map/all_to_all | solution.py:87
  206.1 2.2 reshape.304
  208.5 2.5 iota_compare_fusion.2
  211.2 72.8 %all-to-all-done.3 = bf16[32,768,64]{1,2,0:T(8,128)(2,1)} async-done(((bf16[32,768,64]{1,2,0:T(8,128)(2,1)}), bf16[32,768,64]{1,2,0:T(8,128)(2,1)}, u32[]{:S(2)}, u32[]{:S(2)}) %all-to-all-start.3) | async-done | bytes 3145760 | tf_op jit(solution)/shard_map/all_to_all | solution.py:87
  284.0 6.6 %copy.69 = bf16[32,768,64]{2,1,0:T(8,128)(2,1)} copy(bf16[32,768,64]{1,2,0:T(8,128)(2,1)} %all-to-all-done.3) | data formatting | bytes 6291456 | tf_op jit(solution)/shard_map/all_to_all | solution.py:87
  290.6 36.4 %gather_fusion.1 = bf16[12288,64]{1,0:T(8,128)(2,1)S(1)} fusion(bf16[24576,64]{1,0:T(8,128)(2,1)} %bitcast.37, s32[12288]{0:T(1024)S(1)} %broadcast_clamp_fusion.1), kind=kCustom, calls=%fused_computation.1 | custom fusion | bytes 3194880 | tf_op jit(solution)/shard_map/gather | solution.py:88
  327.1 15.5 %fusion.2 = bf16[256,24,64]{2,1,0:T(8,128)(2,1)} fusion(bf16[256,24,2,64]{3,2,1,0:T(2,128)(2,1)S(1)} %bitcast.39, pred[256,24,2]{2,1,0:T(8,128)(4,1)} %iota_compare_fusion.2), kind=kLoop, calls=%fused_computation.6 | loop fusion | flops 1966080 | bytes 2371584 | tf_op jit(solution)/shard_map/reduce_sum | solution.py:91
  342.6 2.0 copy.71
  344.6 3.7 %fusion.12 = f32[1,256]{1,0:T(1,128)} fusion(bf16[1024,1]{0,1:T(2,128)(2,1)S(1)} %reshape.325, bf16[256,1536]{0,1:T(8,128)(2,1)S(1)} %bitcast.41, bf16[1536,1024]{1,0:T(8,128)(2,1)} %all-gather.4.cloned.1.call-done, f32[1024]{0:T(1024)S(1)} %copy-done.5), kind=kOutput, calls=%fused_computation.26 | convolution fusion | flops 807403520 | bytes 3939328 | tf_op jit(solution)/shard_map/dot_general | solution.py:99
  (40 shorter events, 5.1 us)
Async XLA Ops:
  9.4 21.3 %all-to-all-start = ((s32[32,1,4]{2,1,0:T(1,128)}), s32[32,1,4]{2,1,0:T(1,128)S(1)}, u32[]{:S(2)}, u32[]{:S(2)}) async-start(s32[32,1,4]{2,1,0:T(1,128)} %bitcast), calls=%async_computation | async-start | bytes 32768 | tf_op jit(solution)/shard_map/all_to_all | solution.py:53
  30.7 13.7 %all-to-all-start.1 = ((f32[32,1,256]{2,1,0:T(1,128)}), f32[32,1,256]{2,1,0:T(1,128)S(1)}, u32[]{:S(2)}, u32[]{:S(2)}) async-start(f32[32,1,256]{2,1,0:T(1,128)} %reshape.336), calls=%async_computation.1 | async-start | bytes 65536 | tf_op jit(solution)/shard_map/all_to_all | solution.py:52
  36.4 51.7 %all-gather.6.cloned.1.call-start = ((), (), s32[]{:S(2)}) async-start(), calls=%async_computation.5 | async-start | bytes 4456448 | tf_op jit(solution)/shard_map/all_gather | solution.py:56
  92.7 1.0 copy-start
  92.7 1.0 copy-start.1
  195.2 88.8 %all-to-all-start.3 = ((bf16[32,768,64]{1,2,0:T(8,128)(2,1)}), bf16[32,768,64]{1,2,0:T(8,128)(2,1)}, u32[]{:S(2)}, u32[]{:S(2)}) async-start(bf16[32,768,64]{1,2,0:T(8,128)(2,1)} %copy.68), calls=%async_computation.3 | async-start | bytes 6291456 | tf_op jit(solution)/shard_map/all_to_all | solution.py:87
  205.4 2.8 copy-start.2
  205.5 2.9 copy-start.3
  205.5 3.0 copy-start.4
  205.5 139.1 %all-gather.4.cloned.1.call-start = ((), (), s32[]{:S(2)}) async-start(), calls=%async_computation.4 | async-start | bytes 3244032 | tf_op jit(solution)/shard_map/all_gather | solution.py:95
  327.1 17.6 %copy-start.5 = (f32[1024]{0:T(1024)S(1)}, f32[1024]{0:T(1024)}, u32[]{:S(2)}) copy-start(f32[1024]{0:T(1024)} %param.18) | copy-start | bytes 12292
Sparse Core Ops, SparseCore 0:
  46.9 41.1 all-gather.5
Sparse Core Ops, SparseCore 1:
  209.1 94.5 all-gather.3
